TPU v7x, 512 devices: a whole 4x8x8 slice. The times are simulated.
512 devices in a mesh: rollout: 32 (over z, x), mp: 16 (over y, core).
Axes of the slice: x: 4, y: 8, z: 8, core: 2. Of those that a mesh axis runs over, the one named last changes fastest.
Arguments:
- queries: bfloat16 [128, 256, 8192], P('rollout', None, 'mp'), may hold values from -6 to 6
- keys: bfloat16 [128, 256, 8192], P('rollout', None, 'mp'), may hold values from -0.5 to 0.5
- values_in: bfloat16 [128, 256, 8192], P('rollout', None, 'mp'), may hold values from -64 to 64
- state_in: bfloat16 [128, 64, 16384], P('rollout', 'mp'), may hold values from -6 to 6
- decay_rate: float32 [64], P('mp'), may hold values from 0.0005 to 0.05
- norm_gain: float32 [8192], P('mp'), may hold values from 0.25 to 1.75
- turn_len: int32 [128], P('rollout'), may hold values from 1 to 256, as said below
- relocation: int32 [128], replicated, may hold values from 0 to 127, as said below
Outputs:
- layer_out: bfloat16 [128, 256, 8192], P('rollout', None, 'mp')
- state_out: bfloat16 [128, 64, 16384], P('rollout', 'mp')
Inputs may be any that keep to these rules, and one draw needn't show every extreme that they name: `relocation`: A permutation: entry g is the new position of the conversation at old position g. A conversation keeps its place within its block of 4 positions (new minus old position is a multiple of 4), and the 4 conversations of one block go to 4 different blocks. `turn_len`: the longest turn has exactly 256 tokens.
All inputs are finite; a program needn't handle non-finite values.
Results may differ from a plain program's by a relative error of at most 0.0049.
Values may be sent and summed in bfloat16 or wider, within the bound.
A program may use at most 64 MiB of HBM per device.

v0:
```python
import jax
import jax.numpy as jnp
from jax import lax
from jax.sharding import PartitionSpec as P

epsilon = 1e-05


def per_device(queries, keys, values_in, state_in, decay_rate, norm_gain, turn_len, relocation):
    conv_count, seq_len, feat_width = queries.shape
    head_count = decay_rate.shape[0]
    head_dim = feat_width // head_count
    device = lax.axis_index("rollout")
    my_slots = device * conv_count + jnp.arange(conv_count, dtype=jnp.int32)
    positions = jnp.arange(relocation.shape[0], dtype=jnp.int32)
    source = jnp.sum(
        jnp.where(relocation[None, :] == my_slots[:, None], positions[None, :], 0), axis=1
    )
    shard_rows = lax.all_gather(state_in, "rollout", axis=0, tiled=True)
    row_count = shard_rows.shape[0]
    inside = (source >= 0) & (source < row_count)
    picked = shard_rows[jnp.clip(source, 0, row_count - 1)]
    carried = jnp.where(inside[:, None, None], picked, jnp.zeros_like(state_in))
    q_heads = queries.reshape(conv_count, seq_len, head_count, head_dim)
    k_heads = keys.reshape(conv_count, seq_len, head_count, head_dim)
    v_heads = values_in.reshape(conv_count, seq_len, head_count, head_dim)
    places = jnp.arange(seq_len, dtype=jnp.float32)
    index_row = jnp.arange(seq_len, dtype=jnp.int32)
    live_rows = index_row[None, :] < turn_len[:, None]
    spacing = jnp.maximum(places[:, None] - places[None, :], 0.0)
    decay_grid = jnp.exp(-decay_rate[:, None, None] * spacing[None])
    causal = index_row[:, None] >= index_row[None, :]
    allowed = causal[None, None] & live_rows[:, None, :, None]
    scores = jnp.einsum("cthd,cshd->chts", q_heads, k_heads, preferred_element_type=jnp.float32)
    weights = jnp.where(allowed, scores * decay_grid[None], 0.0).astype(jnp.bfloat16)
    within = jnp.einsum("chts,cshd->cthd", weights, v_heads, preferred_element_type=jnp.float32)
    held_grid = carried.reshape(conv_count, head_count, head_dim, head_dim)
    carried_term = jnp.einsum(
        "cthd,chde->cthe", q_heads, held_grid, preferred_element_type=jnp.float32
    )
    carried_term = (
        carried_term * jnp.exp(-decay_rate[None, :] * (places[:, None] + 1.0))[None, :, :, None]
    )
    attended = jnp.where(live_rows[:, :, None, None], within + carried_term, 0.0)
    square_sum = lax.psum(jnp.sum(attended * attended, axis=(2, 3)), "mp")
    mean_sq = square_sum / (feat_width * lax.axis_size("mp"))
    layer_out = (
        attended.reshape(conv_count, seq_len, feat_width)
        * lax.rsqrt(mean_sq + epsilon)[:, :, None]
        * norm_gain
    ).astype(jnp.bfloat16)
    len_float = turn_len.astype(jnp.float32)
    remain = jnp.maximum(len_float[:, None] - 1.0 - places[None, :], 0.0)
    kweight = jnp.exp(-decay_rate[None, None, :] * remain[:, :, None])
    decayed = jnp.where(live_rows[:, :, None, None], k_heads * kweight[:, :, :, None], 0.0).astype(
        jnp.bfloat16
    )
    update = jnp.einsum("cshd,cshe->chde", decayed, v_heads, preferred_element_type=jnp.float32)
    new_state = (
        jnp.exp(-decay_rate[None, :] * len_float[:, None])[:, :, None, None]
        * held_grid.astype(jnp.float32)
        + update
    )
    state_out = new_state.reshape(conv_count, head_count, head_dim * head_dim).astype(jnp.bfloat16)
    return (layer_out, state_out)


def solution(mesh):
    in_specs = (
        P("rollout", None, "mp"),
        P("rollout", None, "mp"),
        P("rollout", None, "mp"),
        P("rollout", "mp", None),
        P("mp"),
        P("mp"),
        P("rollout"),
        P(),
    )
    out_specs = (P("rollout", None, "mp"), P("rollout", "mp", None))
    return jax.shard_map(
        per_device, mesh=mesh, in_specs=in_specs, out_specs=out_specs, check_vma=False
    )
```

profile of v0, /device:TPU:1, one launch (start us, length us, event | category | flops | bytes accessed | tf_op | source)
XLA Modules:
  0.0 213.2 jit_solution(5771728929906547441)
XLA Ops:
  7.2 0.0 copy-start
  7.2 0.0 copy-start.5
  7.2 0.0 copy-start.4
  7.2 0.0 all-gather.2.cloned.1.call-start
  7.2 0.7 all-gather.2.cloned.1.call-update
  7.9 0.7 neg.9
  8.6 1.5 copy.22
  10.1 0.0 copy-done.5
  10.1 0.0 copy-start.2
  10.1 0.0 copy-done.4
  10.1 0.2 select_reduce_fusion
  10.4 0.1 subtract_maximum_fusion
  10.5 0.1 iota_compare_fusion.1
  10.5 0.1 multiply_exponential_fusion.3
  10.6 0.1 subtract_maximum_fusion.1
  10.7 0.1 multiply_exponential_fusion.2
  10.8 0.1 multiply_exponential_fusion.1
  10.9 0.2 broadcast_and_fusion
  11.1 0.2 multiply_exponential_fusion
  11.3 0.0 copy-done
  11.3 3.9 %fusion.2 = f32[4,4,256,128]{2,3,1,0:T(8,128)} fusion(bf16[4,256,4,128]{1,3,2,0:T(8,128)(2,1)S(1)} %bitcast.46, f32[4,256,256]{2,1,0:T(8,128)S(1)} %multiply_exponential_fusion, pred[4,256,256]{2,1,0:T(8,128)(4,1)S(1)} %broadcast_and_fusion, bf16[4,256,512]{2,1,0:T(8,128)(2,1)} %param.10, bf16[4,256,512]{2,1,0:T(8,128)(2,1)S(1)} %copy-done), kind=kOutput, calls=%fused_computation.8 | convolution fusion | flops 540016640 | bytes 6553600 | tf_op jit(solution)/shard_map/chts,cshd->cthd/dot_general | solution.py:36
  15.2 0.0 copy-done.2
  15.2 147.9 %all-gather.2.cloned.1.call-done = bf16[128,4,16384]{2,1,0:T(4,128)(2,1)} async-done(((bf16[4,4,16384]{2,1,0:T(4,128)(2,1)}), bf16[128,4,16384]{2,1,0:T(4,128)(2,1)}) %all-gather.2.cloned.1.call-update) | async-done | bytes 16777232 | tf_op jit(solution)/shard_map/all_gather | solution.py:19
  163.1 6.8 %gather_fusion = bf16[4,4,16384]{2,1,0:T(4,128)(2,1)S(1)} fusion(bf16[128,4,16384]{2,1,0:T(4,128)(2,1)} %all-gather.2.cloned.1.call-done, s32[1024]{0:T(1024)S(1)} %pad_clamp_fusion), kind=kCustom, calls=%fused_computation | custom fusion | bytes 1048592 | tf_op jit(solution)/shard_map/gather | solution.py:22
  169.9 0.5 gather.6
  170.5 0.0 copy-start.1
  170.5 3.8 %multiply_reduce_fusion = (f32[4,256]{1,0:T(4,128)S(1)}, f32[4,256,4,128]{1,3,2,0:T(8,128)}) fusion(f32[256,4]{0,1:T(4,128)S(1)} %multiply_exponential_fusion.2, bf16[4,4,128,128]{3,2,1,0:T(8,128)(2,1)S(1)} %gather.6, pred[4]{0:T(512)(128)(4,1)S(1)} %compare_and_fusion, f32[4,4,256,128]{2,3,1,0:T(8,128)} %fusion.2, ...), kind=kOutput, calls=%fused_computation.7 | convolution fusion | flops 137100288 | bytes 5776388 | tf_op jit(solution)/shard_map/cthd,chde->cthe/dot_general | solution.py:38
  174.3 0.0 copy-done.1
  174.3 1.9 copy.28
  176.2 23.9 %psum.7 = f32[4,256]{1,0:T(4,128)S(1)} all-reduce(f32[4,256]{1,0:T(4,128)S(1)} %get-tuple-element.2), channel_id=1, replica_groups=mesh['rollout'=32,'mp'=16] {'mp'}, use_global_device_ids=true, to_apply=%region_2.3 | all-reduce | flops 1024 | bytes 8192 | tf_op jit(solution)/shard_map/psum | solution.py:45
  200.2 0.0 copy-start.3
  200.2 2.9 %fusion.3 = bf16[4,4,128,128]{3,2,1,0:T(8,128)(2,1)} fusion(bf16[4,256,4,128]{1,3,2,0:T(8,128)(2,1)} %bitcast.47, f32[4,256,4]{1,2,0:T(4,128)S(1)} %multiply_exponential_fusion.1, pred[4,256]{1,0:T(4,128)(4,1)S(1)} %iota_compare_fusion.1, f32[4,4]{1,0:T(4,128)S(1)} %multiply_exponential_fusion.3, bf16[4,4,128,128]{3,2,1,0:T(8,128)(2,1)} %copy-done.1, ...), kind=kOutput, calls=%fused_computation.10 | convolution fusion | flops 137625600 | bytes 3163204 | tf_op jit(solution)/shard_map/cshd,cshe->chde/dot_general | solution.py:58
  203.1 2.0 convert_element_type.31
  205.1 0.0 copy-done.3
  205.1 1.2 multiply_convert_fusion
  (9 shorter events, 0.1 us)
Async XLA Ops:
  7.2 4.1 %copy-start = (bf16[4,256,512]{2,1,0:T(8,128)(2,1)S(1)}, bf16[4,256,512]{2,1,0:T(8,128)(2,1)}, u32[]{:S(2)}) copy-start(bf16[4,256,512]{2,1,0:T(8,128)(2,1)} %param.8) | copy-start | bytes 3145732
  7.2 2.9 %copy-start.5 = (s32[4]{0:T(128)S(1)}, s32[4]{0:T(128)}, u32[]{:S(2)}) copy-start(s32[4]{0:T(128)} %param.14) | copy-start | bytes 52
  7.2 3.0 %copy-start.4 = (s32[128]{0:T(128)S(1)}, s32[128]{0:T(128)}, u32[]{:S(2)}) copy-start(s32[128]{0:T(128)} %param.15) | copy-start | bytes 1540
  7.2 155.9 %all-gather.2.cloned.1.call-start = ((), (), s32[]{:S(2)}) async-start(), calls=%async_computation | async-start | bytes 17301504 | tf_op jit(solution)/shard_map/all_gather | solution.py:19
  10.1 5.1 %copy-start.2 = (bf16[4,256,512]{1,2,0:T(8,128)(2,1)}, bf16[4,256,512]{1,2,0:T(8,128)(2,1)S(1)}, u32[]{:S(2)}) copy-start(bf16[4,256,512]{1,2,0:T(8,128)(2,1)S(1)} %copy.22) | copy-start | bytes 3145732
  170.5 3.8 %copy-start.1 = (bf16[4,4,128,128]{3,2,1,0:T(8,128)(2,1)}, bf16[4,4,128,128]{3,2,1,0:T(8,128)(2,1)S(1)}, u32[]{:S(2)}) copy-start(bf16[4,4,128,128]{3,2,1,0:T(8,128)(2,1)S(1)} %gather.6) | copy-start | bytes 1572868
  200.2 4.9 %copy-start.3 = (f32[512]{0:T(512)S(1)}, f32[512]{0:T(512)}, u32[]{:S(2)}) copy-start(f32[512]{0:T(512)} %param.13) | copy-start | bytes 6148
Sparse Core Ops, SparseCore 0:
  11.2 151.8 all-gather.1
where the time goes:
time: 214 us; the launch traced here: 213 us
  waiting for transfers between devices  149 us (70%)
  blocking collectives  23.9 us (11%)
  between operations  14.2 us (7%)
  local copies, waits for them, and re-layouts  12.7 us (6%)
  matrix products  10.7 us (5%)
  other arithmetic  2.99 us (1%)
    all_gather x1, waiting for transfers between devices, per_device(): shard_rows = lax.all_gather(state_in, 'rollout', axis=0, tiled=True)  148 us
    psum x1, blocking collectives, per_device(): square_sum = lax.psum(jnp.sum(attended * attended, axis=(2, 3)), 'mp')  23.9 us
    gather x2, local copies, waits for them, and re-layouts, per_device(): picked = shard_rows[jnp.clip(source, 0, row_count - 1)]  7.3 us
  transfers between devices with their start and end apart: 1, of which 1 were waited for; matrix products, arithmetic and copies ran while one was open for 3% of the time, Pallas kernels for 0%

commit v1 on v0

v1 whole, which is shorter than its diff:
```python
import functools

import jax
import jax.numpy as jnp
from jax import lax
from jax.experimental import pallas as pl
from jax.experimental.pallas import tpu as pltpu
from jax.sharding import PartitionSpec as P

EPS = 1e-05
MESH = pl.DeviceIdType.MESH
HD = 128
TURN = 256
CONV = 4
HEADS = 4
WIDTH = HEADS * HD
ROWS = HEADS * HD
CHUNKS = 2
PER = CONV // CHUNKS
NX = 4
HIGH = lax.Precision.HIGHEST


def turn_order(count):
    return sorted(range(count), key=lambda d: -min(d, count - d))


def kernel(
    nb, nm,
    decay_ref, len_ref, src_ref, gain_ref, q_hbm, k_hbm, v_hbm, state_hbm,
    out_hbm, state_out_hbm,
    q, k, v, att, upd, grid, qdec, outg, carr, wide, sums, out, sout,
    load_sem, a_send, a_recv, b_send, b_recv, m_send, m_recv, out_sem, *gath,
):
    me = lax.axis_index("rollout")
    m = lax.axis_index("mp")
    nx = min(NX, nb)
    nz = nb // nx
    z = me // nx
    x = lax.rem(me, nx)
    rows = ROWS // nb
    peers = []
    for dz in turn_order(nz):
        for dx in turn_order(nx):
            if dz or dx:
                peers.append(lax.rem(z + dz, nz) * nx + lax.rem(x + dx, nx))

    barrier = pltpu.get_barrier_semaphore()
    for t in peers:
        pl.semaphore_signal(barrier, inc=1, device_id=(t, m), device_id_type=MESH)
    for d in range(1, nm):
        pl.semaphore_signal(
            barrier, inc=1, device_id=(me, lax.rem(m + d, nm)), device_id_type=MESH
        )
    loads = [
        pltpu.make_async_copy(hbm, vmem, load_sem.at[n])
        for n, (hbm, vmem) in enumerate(((k_hbm, k), (v_hbm, v), (q_hbm, q)))
    ]
    for copy in loads:
        copy.start()
    pl.semaphore_wait(barrier, nb - 1 + nm - 1)

    def piece(t):
        return pl.ds(pl.multiple_of(t * rows, rows), rows)

    def spread(c, t):
        return state_hbm.at[pl.ds(c * PER, PER), piece(t), :], gath[c].at[me]

    def deliver(c, t):
        return outg.at[c, t], carr.at[pl.ds(c * PER, PER), piece(me), :]

    def send_all(c, which, send_sem, recv_sem):
        for t in peers:
            source, target = which(c, t)
            pltpu.make_async_remote_copy(
                src_ref=source, dst_ref=target, send_sem=send_sem.at[c],
                recv_sem=recv_sem.at[c], device_id=(t, m), device_id_type=MESH,
            ).start()
        source, target = which(c, me)
        pltpu.make_async_copy(source, target, recv_sem.at[c]).start()

    def wait_bytes(ref, sem):
        pltpu.make_async_copy(ref, ref, sem).wait()

    for c in range(CHUNKS):
        send_all(c, spread, a_send, a_recv)

    t_idx = lax.broadcasted_iota(jnp.int32, (TURN, TURN), 0)
    s_idx = lax.broadcasted_iota(jnp.int32, (TURN, TURN), 1)
    spacing = jnp.maximum(t_idx - s_idx, 0).astype(jnp.float32)
    causal = t_idx >= s_idx
    row_i = lax.broadcasted_iota(jnp.int32, (TURN, HD), 0)
    row_f = row_i.astype(jnp.float32)
    for h in range(HEADS):
        grid[h] = jnp.where(causal, jnp.exp(-decay_ref[h] * spacing), 0.0)
        qdec[h] = jnp.exp(-decay_ref[h] * (row_f + 1.0))
    for copy in loads:
        copy.wait()

    def local(j, _):
        length = len_ref[j]
        live = row_i < length
        remain = jnp.maximum(length.astype(jnp.float32) - 1.0 - row_f, 0.0)
        for h in range(HEADS):
            cols = slice(h * HD, (h + 1) * HD)
            qh, kh, vh = q[j, :, cols], k[j, :, cols], v[j, :, cols]
            scores = lax.dot_general(
                qh, kh, (((1,), (1,)), ((), ())), preferred_element_type=jnp.float32
            )
            weights = (scores * grid[h]).astype(jnp.bfloat16)
            att[j, :, cols] = jnp.dot(weights, vh, preferred_element_type=jnp.float32)
            kdec = jnp.where(
                live, kh.astype(jnp.float32) * jnp.exp(-decay_ref[h] * remain), 0.0
            ).astype(jnp.bfloat16)
            upd[j, h] = lax.dot_general(
                kdec, vh, (((0,), (0,)), ((), ())), preferred_element_type=jnp.float32
            )
        return 0

    lax.fori_loop(0, CONV, local, 0)

    for c in range(CHUNKS):
        wait_bytes(gath[c], a_recv.at[c])

        def pick(d, _):
            for jj in range(PER):
                outg[c, d, jj] = gath[c][src_ref[d * CONV + c * PER + jj], jj]
            return 0

        lax.fori_loop(0, nb, pick, 0)
        send_all(c, deliver, b_send, b_recv)

    for c in range(CHUNKS):
        wait_bytes(carr.at[pl.ds(c * PER, PER)], b_recv.at[c])

        def finish(jj, _):
            j = c * PER + jj
            length = len_ref[j]
            live = row_i < length
            wide[0] = carr[j].astype(jnp.float32)
            square = jnp.zeros((TURN, HD), jnp.float32)
            for h in range(HEADS):
                cols = slice(h * HD, (h + 1) * HD)
                held = wide[0, pl.ds(h, HD, stride=HEADS), :]
                term = jnp.dot(
                    q[j, :, cols], held.astype(jnp.bfloat16), preferred_element_type=jnp.float32
                )
                a = jnp.where(live, att[j, :, cols] + term * qdec[h], 0.0)
                att[j, :, cols] = a
                square = square + a * a
                keep = jnp.exp(
                    jnp.full((HD, HD), -decay_ref[h] * length.astype(jnp.float32), jnp.float32)
                )
                wide[1, pl.ds(h, HD, stride=HEADS), :] = keep * held + upd[j, h]
            sout[j] = wide[1].astype(jnp.bfloat16)
            row = lax.dot_general(
                jnp.ones((8, HD), jnp.float32), square, (((1,), (1,)), ((), ())),
                preferred_element_type=jnp.float32, precision=HIGH,
            )
            sums[c, m, pl.ds(jj, 1), :] = row[0:1]
            return 0

        for jj in range(PER):
            finish(jj, 0)
        for d in range(1, nm):
            pltpu.make_async_remote_copy(
                src_ref=sums.at[c, m], dst_ref=sums.at[c, m], send_sem=m_send.at[c, d],
                recv_sem=m_recv.at[c, d], device_id=(me, lax.rem(m + d, nm)),
                device_id_type=MESH,
            ).start()
        pltpu.make_async_copy(
            sout.at[pl.ds(c * PER, PER)], state_out_hbm.at[pl.ds(c * PER, PER)], out_sem.at[0, c]
        ).start()

    for c in range(CHUNKS):
        for d in range(1, nm):
            pltpu.make_async_remote_copy(
                src_ref=sums.at[c, m], dst_ref=sums.at[c, m], send_sem=m_send.at[c, d],
                recv_sem=m_recv.at[c, d], device_id=(me, lax.rem(m + d, nm)),
                device_id_type=MESH,
            ).wait()
        for jj in range(PER):
            j = c * PER + jj
            total = lax.dot_general(
                sums[c, :, jj, :], jnp.ones((nm, HD), jnp.float32), (((0,), (0,)), ((), ())),
                preferred_element_type=jnp.float32, precision=HIGH,
            )
            scale = lax.rsqrt(total / (nm * WIDTH) + EPS)
            for h in range(HEADS):
                cols = slice(h * HD, (h + 1) * HD)
                out[j, :, cols] = (att[j, :, cols] * scale * gain_ref[:, cols]).astype(jnp.bfloat16)
        pltpu.make_async_copy(
            out.at[pl.ds(c * PER, PER)], out_hbm.at[pl.ds(c * PER, PER)], out_sem.at[1, c]
        ).start()

    for c in range(CHUNKS):
        wait_bytes(gath[c].at[pl.ds(0, nb - 1)], a_send.at[c])
        wait_bytes(outg.at[c, pl.ds(0, nb - 1)], b_send.at[c])
        wait_bytes(sout.at[pl.ds(c * PER, PER)], out_sem.at[0, c])
        wait_bytes(out.at[pl.ds(c * PER, PER)], out_sem.at[1, c])


def per_device(nb, nm, queries, keys, values_in, state_in, decay_rate, norm_gain, turn_len, relocation):
    convs = relocation.shape[0]
    places = jnp.arange(convs, dtype=jnp.int32)
    src_block = jnp.sum(
        jnp.where(relocation[None, :] == places[:, None], places[None, :] // CONV, 0), axis=1
    ).astype(jnp.int32)
    state = state_in.reshape(CONV, HEADS, HD, HD).transpose(0, 2, 1, 3).reshape(CONV, ROWS, HD)
    rows = ROWS // nb
    bf16, f32 = jnp.bfloat16, jnp.float32
    smem = pl.BlockSpec(memory_space=pltpu.SMEM)
    hbm = pl.BlockSpec(memory_space=pl.ANY)
    layer_out, state_out = pl.pallas_call(
        functools.partial(kernel, nb, nm),
        out_shape=(
            jax.ShapeDtypeStruct((CONV, TURN, WIDTH), bf16),
            jax.ShapeDtypeStruct((CONV, ROWS, HD), bf16),
        ),
        in_specs=[smem, smem, smem, pl.BlockSpec(memory_space=pltpu.VMEM), hbm, hbm, hbm, hbm],
        out_specs=(hbm, hbm),
        scratch_shapes=[
            pltpu.VMEM((CONV, TURN, WIDTH), bf16),
            pltpu.VMEM((CONV, TURN, WIDTH), bf16),
            pltpu.VMEM((CONV, TURN, WIDTH), bf16),
            pltpu.VMEM((CONV, TURN, WIDTH), f32),
            pltpu.VMEM((CONV, HEADS, HD, HD), f32),
            pltpu.VMEM((HEADS, TURN, TURN), f32),
            pltpu.VMEM((HEADS, TURN, HD), f32),
            pltpu.VMEM((CHUNKS, nb, PER, rows, HD), bf16),
            pltpu.VMEM((CONV, ROWS, HD), bf16),
            pltpu.VMEM((2, ROWS, HD), f32),
            pltpu.VMEM((CHUNKS, nm, PER, TURN), f32),
            pltpu.VMEM((CONV, TURN, WIDTH), bf16),
            pltpu.VMEM((CONV, ROWS, HD), bf16),
            pltpu.SemaphoreType.DMA((3,)),
            pltpu.SemaphoreType.DMA((CHUNKS,)),
            pltpu.SemaphoreType.DMA((CHUNKS,)),
            pltpu.SemaphoreType.DMA((CHUNKS,)),
            pltpu.SemaphoreType.DMA((CHUNKS,)),
            pltpu.SemaphoreType.DMA((CHUNKS, nm)),
            pltpu.SemaphoreType.DMA((CHUNKS, nm)),
            pltpu.SemaphoreType.DMA((2, CHUNKS)),
        ] + [pltpu.VMEM((nb, PER, rows, HD), bf16)] * CHUNKS,
        compiler_params=pltpu.CompilerParams(
            collective_id=0, has_side_effects=True, vmem_limit_bytes=58 << 20
        ),
    )(
        decay_rate, turn_len, src_block, norm_gain.reshape(1, WIDTH),
        queries, keys, values_in, state,
    )
    state_out = state_out.reshape(CONV, HD, HEADS, HD).transpose(0, 2, 1, 3)
    return layer_out, state_out.reshape(CONV, HEADS, HD * HD)


def solution(mesh):
    nb, nm = mesh.shape["rollout"], mesh.shape["mp"]
    in_specs = (
        P("rollout", None, "mp"),
        P("rollout", None, "mp"),
        P("rollout", None, "mp"),
        P("rollout", "mp", None),
        P("mp"),
        P("mp"),
        P("rollout"),
        P(),
    )
    out_specs = (P("rollout", None, "mp"), P("rollout", "mp", None))
    return jax.shard_map(
        functools.partial(per_device, nb, nm),
        mesh=mesh, in_specs=in_specs, out_specs=out_specs, check_vma=False,
    )
```

time: 214 us -> 55.4 us (0.26)
  waiting for transfers between devices: 149 us -> 0 us
  Pallas kernels: 0 us -> 50.2 us
  blocking collectives: 23.9 us -> 0 us
  between operations: 14.2 us -> 0.66 us
  matrix products: 10.7 us -> 0 us
  local copies, waits for them, and re-layouts: 12.7 us -> 3.75 us
  other arithmetic: 2.99 us -> 0.63 us
    all_gather x1 -> x0, waiting for transfers between devices: 148 us -> none  [per_device(): shard_rows = lax.all_gather(state_in, 'rollout', axis=0, tiled=True)]
    pallas_call x0 -> x1, Pallas kernels: none -> 50.2 us  [per_device(): pl.pallas_call(functools.partial(kernel, nb, nm), out_shape=(jax.ShapeDty...]
    psum x1 -> x0, blocking collectives: 23.9 us -> none  [per_device(): square_sum = lax.psum(jnp.sum(attended * attended, axis=(2, 3)), 'mp')]
    dot_general x3 -> x0, matrix products: 10.7 us -> none  [the longest x1 3.9 us: per_device(): jnp.einsum('chts,cshd->cthd', weights, v_heads, preferred_element_type=jn...]
    gather x2 -> x0, local copies, waits for them, and re-layouts: 7.3 us -> none  [per_device(): picked = shard_rows[jnp.clip(source, 0, row_count - 1)]]
    unnamed x13 -> x6, local copies, waits for them, and re-layouts: 1.51 us -> 3.75 us
  transfers between devices with their start and end apart: 1 -> 0, of which waited for: 1 -> 0; matrix products, arithmetic and copies ran while one was open for 3% -> 0% of each run, Pallas kernels for 0% -> 0%
where the time goes in v1:
time: 55.4 us; the launch traced here: 55.2 us
  Pallas kernels  50.2 us (91%)
  local copies, waits for them, and re-layouts  3.75 us (7%)
  between operations  0.66 us (1%)
  other arithmetic  0.63 us (1%)
    pallas_call x1, Pallas kernels, per_device(): pl.pallas_call(functools.partial(kernel, nb, nm), out_shape=(jax.ShapeDty...  50.2 us
    unnamed x6, local copies, waits for them, and re-layouts  3.75 us

profile of v1, /device:TPU:1, one launch (start us, length us, event | category | flops | bytes accessed | tf_op | source)
XLA Modules:
  0.0 55.2 jit_solution(11320729009142734483)
XLA Ops:
  0.6 0.0 copy-start.1
  0.6 0.6 %copy-done.1 = s32[128]{0:T(128)S(1)} copy-done((s32[128]{0:T(128)S(1)}, s32[128]{0:T(128)}, u32[]{:S(2)}) %copy-start.1) | copy-done | bytes 536
  1.3 0.6 %select_reduce_fusion.src_ref = s32[128]{0:T(128)} fusion(s32[128]{0:T(128)S(1)} %and_select_fusion, s32[128]{0:T(128)S(1)} %copy-done.1), kind=kLoop, calls=%fused_computation | loop fusion | flops 49024 | bytes 1536 | tf_op jit(solution)/shard_map/reduce_sum | solution.py:206
  1.9 50.2 %shard_map.95 = (bf16[4,256,512]{2,1,0:T(8,128)(2,1)}, bf16[4,512,128]{2,1,0:T(8,128)(2,1)}) custom-call(f32[4]{0:T(128)} %decay_ref.1, s32[4]{0:T(128)} %len_ref.1, s32[128]{0:T(128)} %select_reduce_fusion.src_ref, f32[1,512]{1,0:T(1,128)} %bitcast.13, bf16[4,256,512]{2,1,0:T(8,128)(2,1)} %q_hbm.1, bf16[4,256,512]{2,1,0:T(8,128)(2,1)} %k_hbm.1, ...), custom_call_target="tpu_custom_call" | custom-call | tf_op jit(solution)/shard_map/pallas_call | solution.py:214
  52.1 0.0 copy-start
  52.1 2.3 %copy.16 = bf16[4,256,512]{2,1,0:T(8,128)(2,1)} copy(bf16[4,256,512]{2,1,0:T(8,128)(2,1)} %get-tuple-element.8) | data formatting | bytes 2097152
  54.4 0.0 copy-done
  54.4 0.8 %copy.17 = bf16[4,4,16384]{2,1,0:T(4,128)(2,1)} copy(bf16[4,4,16384]{2,1,0:T(4,128)(2,1)S(1)} %bitcast.11) | data formatting | bytes 1048576
  (1 shorter events, 0.0 us)
Async XLA Ops:
  0.6 0.7 %copy-start.1 = (s32[128]{0:T(128)S(1)}, s32[128]{0:T(128)}, u32[]{:S(2)}) copy-start(s32[128]{0:T(128)} %param.15) | copy-start | bytes 1540
  52.1 2.3 %copy-start = (bf16[4,512,128]{2,1,0:T(8,128)(2,1)S(1)}, bf16[4,512,128]{2,1,0:T(8,128)(2,1)}, u32[]{:S(2)}) copy-start(bf16[4,512,128]{2,1,0:T(8,128)(2,1)} %get-tuple-element.5) | copy-start | bytes 1572868

commit v2 on v1

v2 whole, which is shorter than its diff:
```python
import functools

import jax
import jax.numpy as jnp
from jax import lax
from jax.experimental import pallas as pl
from jax.experimental.pallas import tpu as pltpu
from jax.sharding import PartitionSpec as P

EPS = 1e-05
MESH = pl.DeviceIdType.MESH
HD = 128
TURN = 256
CONV = 4
HEADS = 4
WIDTH = HEADS * HD
ROWS = HEADS * HD
CHUNKS = 2
ORDER = [(dz, dx) for dz in (4, 3, 5, 2, 6, 1, 7, 0) for dx in (2, 1, 3, 0) if dz or dx]
PER = CONV // CHUNKS
NX = 4
HIGH = lax.Precision.HIGHEST


def wait_bytes(ref, sem):
    pltpu.make_async_copy(ref, ref, sem).wait()


def kernel(
    nx, nz, nm,
    decay_hbm, len_hbm, reloc_hbm, gain_hbm, q_hbm, k_hbm, v_hbm, state_hbm,
    out, sout,
    decay_ref, len_ref, src_ref, src_row, reloc_ref, gain_ref,
    q, k, v, att, upd, grid, qdec, outg, carr, wide, sums,
    small_sem, load_sem, a_sem, b_sem, m_sem, *gath,
):
    nb = nz * nx
    me = lax.axis_index("rollout")
    m = lax.axis_index("mp")
    z = me // nx
    x = lax.rem(me, nx)
    rows = ROWS // nb

    def peer(dz, dx):
        return lax.rem(z + dz, nz) * nx + lax.rem(x + dx, nx)

    peers = [peer(dz, dx) for dz, dx in ORDER if dz < nz and dx < nx]
    barrier = pltpu.get_barrier_semaphore()
    for t in reversed(peers):
        pl.semaphore_signal(barrier, inc=1, device_id=(t, m), device_id_type=MESH)
    for d in range(1, nm):
        pl.semaphore_signal(barrier, inc=1, device_id=(me, lax.rem(m + d, nm)), device_id_type=MESH)

    def piece(t):
        return pl.ds(pl.multiple_of(t * rows, rows), rows)

    def convs(c):
        return pl.ds(c * PER, PER)

    loads = [
        pltpu.make_async_copy(source, target, small_sem.at[n])
        for n, (source, target) in enumerate((
            (reloc_hbm, reloc_ref), (decay_hbm, decay_ref), (len_hbm, len_ref), (gain_hbm, gain_ref),
        ))
    ] + [
        pltpu.make_async_copy(source, target, load_sem.at[n])
        for n, (source, target) in enumerate(((k_hbm, k), (v_hbm, v), (q_hbm, q)))
    ]
    for copy in loads:
        copy.start()
    pl.semaphore_wait(barrier, nb - 1 + nm - 1)

    for c in range(CHUNKS):
        for t in peers:
            pltpu.make_async_remote_copy(
                src_ref=state_hbm.at[convs(c), piece(t), :], dst_ref=gath[c].at[me],
                send_sem=a_sem.at[0, c], recv_sem=a_sem.at[1, c],
                device_id=(t, m), device_id_type=MESH,
            ).start()
        pltpu.make_async_copy(
            state_hbm.at[convs(c), piece(me), :], gath[c].at[me], a_sem.at[1, c]
        ).start()

    for copy in loads[:4]:
        copy.wait()
    places = src_row.shape[1]
    came = jnp.broadcast_to(reloc_ref[...], (places, places)).T
    old = lax.broadcasted_iota(jnp.int32, (places, places), 0) // CONV
    place = lax.broadcasted_iota(jnp.int32, (places, places), 1)
    src_row[...] = jnp.max(jnp.where(came == place, old, 0), axis=0, keepdims=True)
    to_scalars = pltpu.make_async_copy(src_row, src_ref, small_sem.at[4])
    to_scalars.start()

    t_idx = lax.broadcasted_iota(jnp.int32, (TURN, TURN), 0)
    s_idx = lax.broadcasted_iota(jnp.int32, (TURN, TURN), 1)
    spacing = jnp.maximum(t_idx - s_idx, 0).astype(jnp.float32)
    causal = t_idx >= s_idx
    row_i = lax.broadcasted_iota(jnp.int32, (TURN, HD), 0)
    row_f = row_i.astype(jnp.float32)
    for h in range(HEADS):
        grid[h] = jnp.where(causal, jnp.exp(-decay_ref[h] * spacing), 0.0)
        qdec[h] = jnp.exp(-decay_ref[h] * (row_f + 1.0))
    for copy in loads[4:]:
        copy.wait()
    to_scalars.wait()

    def local(j, _):
        length = len_ref[j]
        live = row_i < length
        remain = jnp.maximum(length.astype(jnp.float32) - 1.0 - row_f, 0.0)
        for h in range(HEADS):
            cols = slice(h * HD, (h + 1) * HD)
            qh, kh, vh = q[j, :, cols], k[j, :, cols], v[j, :, cols]
            scores = lax.dot_general(
                qh, kh, (((1,), (1,)), ((), ())), preferred_element_type=jnp.float32
            )
            weights = (scores * grid[h]).astype(jnp.bfloat16)
            att[j, :, cols] = jnp.dot(weights, vh, preferred_element_type=jnp.float32)
            kdec = jnp.where(
                live, kh.astype(jnp.float32) * jnp.exp(-decay_ref[h] * remain), 0.0
            ).astype(jnp.bfloat16)
            upd[j, h] = lax.dot_general(
                kdec, vh, (((0,), (0,)), ((), ())), preferred_element_type=jnp.float32
            )
        return 0

    lax.fori_loop(0, CONV, local, 0)

    for c in range(CHUNKS):
        wait_bytes(gath[c], a_sem.at[1, c])

        def pick(d, _):
            for jj in range(PER):
                outg[c, d, jj] = gath[c][src_ref[0, d * CONV + c * PER + jj], jj]
            return 0

        lax.fori_loop(0, nb, pick, 0, unroll=4)
        for t in peers:
            pltpu.make_async_remote_copy(
                src_ref=outg.at[c, t], dst_ref=carr.at[convs(c), piece(me), :],
                send_sem=b_sem.at[0, c], recv_sem=b_sem.at[1, c],
                device_id=(t, m), device_id_type=MESH,
            ).start()
        pltpu.make_async_copy(
            outg.at[c, me], carr.at[convs(c), piece(me), :], b_sem.at[1, c]
        ).start()

    def read_carried(j):
        wide[0] = carr[j].astype(jnp.float32)

    def head(h):
        return wide[0, pl.ds(h, HD, stride=HEADS), :]

    def finish(c):
        wait_bytes(carr.at[convs(c)], b_sem.at[1, c])
        for jj in range(PER):
            j = c * PER + jj
            live = row_i < len_ref[j]
            read_carried(j)
            square = jnp.zeros((TURN, HD), jnp.float32)
            for h in range(HEADS):
                cols = slice(h * HD, (h + 1) * HD)
                term = jnp.dot(
                    q[j, :, cols], head(h).astype(jnp.bfloat16), preferred_element_type=jnp.float32
                )
                a = jnp.where(live, att[j, :, cols] + term * qdec[h], 0.0)
                att[j, :, cols] = a
                square = square + a * a
            high = square.astype(jnp.bfloat16)
            low = (square - high.astype(jnp.float32)).astype(jnp.bfloat16)
            row = lax.dot_general(
                jnp.ones((8, 2 * HD), jnp.bfloat16), jnp.concatenate([high, low], axis=1),
                (((1,), (1,)), ((), ())), preferred_element_type=jnp.float32,
            )
            sums[c, m, pl.ds(jj, 1), :] = row[0:1]
        for d in range(1, nm):
            pltpu.make_async_remote_copy(
                src_ref=sums.at[c, m], dst_ref=sums.at[c, m], send_sem=m_sem.at[0, c],
                recv_sem=m_sem.at[1, c], device_id=(me, lax.rem(m + d, nm)), device_id_type=MESH,
            ).start()

    def update(c):
        for jj in range(PER):
            j = c * PER + jj
            length = len_ref[j].astype(jnp.float32)
            read_carried(j)
            for h in range(HEADS):
                keep = jnp.exp(jnp.full((HD, HD), -decay_ref[h] * length, jnp.float32))
                wide[1, pl.ds(h, HD, stride=HEADS), :] = keep * head(h) + upd[j, h]
            sout[j] = wide[1].astype(jnp.bfloat16)

    def normalize(c):
        wait_bytes(sums.at[c, pl.ds(0, nm - 1)], m_sem.at[1, c])
        for jj in range(PER):
            j = c * PER + jj
            total = lax.dot_general(
                sums[c, :, jj, :], jnp.ones((nm, HD), jnp.float32), (((0,), (0,)), ((), ())),
                preferred_element_type=jnp.float32, precision=HIGH,
            )
            scale = lax.rsqrt(total / (nm * WIDTH) + EPS)
            for h in range(HEADS):
                cols = slice(h * HD, (h + 1) * HD)
                out[j, :, cols] = (att[j, :, cols] * scale * gain_ref[:, cols]).astype(jnp.bfloat16)

    for c in range(CHUNKS):
        finish(c)
    for c in range(CHUNKS):
        update(c)
    for c in range(CHUNKS):
        normalize(c)

    for c in range(CHUNKS):
        wait_bytes(gath[c].at[pl.ds(0, nb - 1)], a_sem.at[0, c])
        wait_bytes(outg.at[c, pl.ds(0, nb - 1)], b_sem.at[0, c])
        wait_bytes(sums.at[c, pl.ds(0, nm - 1)], m_sem.at[0, c])


def store_kernel(out, sout, out_hbm, sout_hbm, sems):
    copies = [
        pltpu.make_async_copy(out, out_hbm, sems.at[0]),
        pltpu.make_async_copy(sout, sout_hbm, sems.at[1]),
    ]
    for copy in copies:
        copy.start()
    for copy in copies:
        copy.wait()


def per_device(nb, nm, queries, keys, values_in, state_in, decay_rate, norm_gain, turn_len, relocation):
    state = state_in.reshape(CONV, HEADS, HD, HD).transpose(0, 2, 1, 3).reshape(CONV, ROWS, HD)
    nx = min(NX, nb)
    nz = nb // nx
    rows = ROWS // nb
    places = relocation.shape[0]
    bf16, f32 = jnp.bfloat16, jnp.float32
    anywhere = pl.BlockSpec(memory_space=pl.ANY)
    in_vmem = pl.BlockSpec(memory_space=pltpu.VMEM)
    operands = [
        pltpu.with_memory_space_constraint(a, pltpu.HBM)
        for a in (
            decay_rate, turn_len, relocation.reshape(1, places), norm_gain.reshape(1, WIDTH),
            queries, keys, values_in, state,
        )
    ]
    layer_out, state_out = pl.pallas_call(
        functools.partial(kernel, nx, nz, nm),
        out_shape=(
            pltpu.VMEM((CONV, TURN, WIDTH), bf16),
            pltpu.VMEM((CONV, ROWS, HD), bf16),
        ),
        in_specs=[anywhere] * 8,
        out_specs=(in_vmem, in_vmem),
        scratch_shapes=[
            pltpu.SMEM((HEADS,), f32),
            pltpu.SMEM((CONV,), jnp.int32),
            pltpu.SMEM((1, places), jnp.int32),
            pltpu.VMEM((1, places), jnp.int32),
            pltpu.VMEM((1, places), jnp.int32),
            pltpu.VMEM((1, WIDTH), f32),
            pltpu.VMEM((CONV, TURN, WIDTH), bf16),
            pltpu.VMEM((CONV, TURN, WIDTH), bf16),
            pltpu.VMEM((CONV, TURN, WIDTH), bf16),
            pltpu.VMEM((CONV, TURN, WIDTH), f32),
            pltpu.VMEM((CONV, HEADS, HD, HD), f32),
            pltpu.VMEM((HEADS, TURN, TURN), f32),
            pltpu.VMEM((HEADS, TURN, HD), f32),
            pltpu.VMEM((CHUNKS, nb, PER, rows, HD), bf16),
            pltpu.VMEM((CONV, ROWS, HD), bf16),
            pltpu.VMEM((2, ROWS, HD), f32),
            pltpu.VMEM((CHUNKS, nm, PER, TURN), f32),
            pltpu.SemaphoreType.DMA((5,)),
            pltpu.SemaphoreType.DMA((3,)),
        ]
        + [pltpu.SemaphoreType.DMA((2, CHUNKS))] * 3
        + [pltpu.VMEM((nb, PER, rows, HD), bf16)] * CHUNKS,
        compiler_params=pltpu.CompilerParams(
            collective_id=0, has_side_effects=True, vmem_limit_bytes=40 << 20
        ),
    )(*operands)
    layer_out, state_out = pl.pallas_call(
        store_kernel,
        out_shape=(
            jax.ShapeDtypeStruct((CONV, TURN, WIDTH), bf16),
            jax.ShapeDtypeStruct((CONV, ROWS, HD), bf16),
        ),
        in_specs=[anywhere] * 2,
        out_specs=(anywhere, anywhere),
        scratch_shapes=[pltpu.SemaphoreType.DMA((2,))],
    )(*(pltpu.with_memory_space_constraint(a, pltpu.VMEM) for a in (layer_out, state_out)))
    state_out = state_out.reshape(CONV, HD, HEADS, HD).transpose(0, 2, 1, 3)
    return layer_out, state_out.reshape(CONV, HEADS, HD * HD)


def solution(mesh):
    nb, nm = mesh.shape["rollout"], mesh.shape["mp"]
    in_specs = (
        P("rollout", None, "mp"),
        P("rollout", None, "mp"),
        P("rollout", None, "mp"),
        P("rollout", "mp", None),
        P("mp"),
        P("mp"),
        P("rollout"),
        P(),
    )
    out_specs = (P("rollout", None, "mp"), P("rollout", "mp", None))
    return jax.shard_map(
        functools.partial(per_device, nb, nm),
        mesh=mesh, in_specs=in_specs, out_specs=out_specs, check_vma=False,
    )
```

time: 55.4 us -> 49.8 us (0.90)
  local copies, waits for them, and re-layouts: 3.75 us -> 0 us
  Pallas kernels: 50.2 us -> 49 us
  other arithmetic: 0.63 us -> 0 us
    unnamed x6 -> x0, local copies, waits for them, and re-layouts: 3.75 us -> none
    pallas_call x1 -> x2, Pallas kernels: 50.2 us -> 49 us  [the longest x1 47.9 us: per_device(): pl.pallas_call(functools.partial(kernel, nx, nz, nm), out_shape=(pltpu.VM...]
    reduce_sum x1 -> x0, other arithmetic: 0.62 us -> none  [per_device(): jnp.sum(jnp.where(relocation[None, :] == places[:, None], places[None, :]...]
where the time goes in v2:
time: 49.8 us; the launch traced here: 49.7 us
  Pallas kernels  49 us (98%)
  between operations  0.64 us (1%)
    pallas_call x1, Pallas kernels, per_device(): pl.pallas_call(functools.partial(kernel, nx, nz, nm), out_shape=(pltpu.VM...  47.9 us
    pallas_call x1, Pallas kernels, per_device(): pl.pallas_call(store_kernel, out_shape=(jax.ShapeDtypeStruct((CONV, TURN,...  1.16 us

profile of v2, /device:TPU:1, one launch (start us, length us, event | category | flops | bytes accessed | tf_op | source)
XLA Modules:
  0.0 49.7 jit_solution(6457542175378386319)
XLA Ops:
  0.6 47.9 %shard_map.95 = (bf16[4,256,512]{2,1,0:T(8,128)(2,1)S(1)}, bf16[4,512,128]{2,1,0:T(8,128)(2,1)S(1)}) custom-call(f32[4]{0:T(128)} %decay_hbm.1, s32[4]{0:T(128)} %len_hbm.1, s32[1,128]{1,0:T(1,128)} %bitcast.14, f32[1,512]{1,0:T(1,128)} %bitcast.13, bf16[4,256,512]{2,1,0:T(8,128)(2,1)} %q_hbm.1, bf16[4,256,512]{2,1,0:T(8,128)(2,1)} %k_hbm.1, ...), custom_call_target="tpu_custom_call" | custom-call | tf_op jit(solution)/shard_map/pallas_call | solution.py:245
  48.5 1.2 %shard_map.96 = (bf16[4,256,512]{2,1,0:T(8,128)(2,1)}, bf16[4,512,128]{2,1,0:T(8,128)(2,1)}) custom-call(bf16[4,256,512]{2,1,0:T(8,128)(2,1)S(1)} %get-tuple-element.6.out, bf16[4,512,128]{2,1,0:T(8,128)(2,1)S(1)} %get-tuple-element.7.sout), custom_call_target="tpu_custom_call" | custom-call | tf_op jit(solution)/shard_map/pallas_call | solution.py:280

commit v3 on v2

--- a/solution.py
+++ b/solution.py
@@ -15,9 +15,11 @@
 HEADS = 4
 WIDTH = HEADS * HD
 ROWS = HEADS * HD
-CHUNKS = 2
+SIZES = (2, 2)
+STARTS = (0, 2)
+CHUNKS = len(SIZES)
+ZORDER = (4, 3, 5, 2, 6, 1, 7)
 ORDER = [(dz, dx) for dz in (4, 3, 5, 2, 6, 1, 7, 0) for dx in (2, 1, 3, 0) if dz or dx]
-PER = CONV // CHUNKS
 NX = 4
 HIGH = lax.Precision.HIGHEST
 
@@ -31,9 +33,10 @@
     decay_hbm, len_hbm, reloc_hbm, gain_hbm, q_hbm, k_hbm, v_hbm, state_hbm,
     out, sout,
     decay_ref, len_ref, src_ref, src_row, reloc_ref, gain_ref,
-    q, k, v, att, upd, grid, qdec, outg, carr, wide, sums,
-    small_sem, load_sem, a_sem, b_sem, m_sem, *gath,
+    q, k, v, att, upd, grid, qdec, carr, wide,
+    small_sem, load_sem, a_sem, b_sem, m_sem, row_sem, *slots,
 ):
+    gath, outg, sums = slots[:CHUNKS], slots[CHUNKS:2 * CHUNKS], slots[2 * CHUNKS:]
     nb = nz * nx
     me = lax.axis_index("rollout")
     m = lax.axis_index("mp")
@@ -44,9 +47,12 @@
     def peer(dz, dx):
         return lax.rem(z + dz, nz) * nx + lax.rem(x + dx, nx)
 
-    peers = [peer(dz, dx) for dz, dx in ORDER if dz < nz and dx < nx]
+    column = [peer(dz, 0) for dz in ZORDER if dz < nz]
+    row = [peer(0, dx) for dx in (2, 1, 3) if dx < nx]
+    rest = [peer(dz, dx) for dz, dx in ORDER if 0 < dz < nz and 0 < dx < nx]
+    peers = column + row + rest
     barrier = pltpu.get_barrier_semaphore()
-    for t in reversed(peers):
+    for t in column + row:
         pl.semaphore_signal(barrier, inc=1, device_id=(t, m), device_id_type=MESH)
     for d in range(1, nm):
         pl.semaphore_signal(barrier, inc=1, device_id=(me, lax.rem(m + d, nm)), device_id_type=MESH)
@@ -55,7 +61,7 @@
         return pl.ds(pl.multiple_of(t * rows, rows), rows)
 
     def convs(c):
-        return pl.ds(c * PER, PER)
+        return pl.ds(STARTS[c], SIZES[c])
 
     loads = [
         pltpu.make_async_copy(source, target, small_sem.at[n])
@@ -66,12 +72,14 @@
         pltpu.make_async_copy(source, target, load_sem.at[n])
         for n, (source, target) in enumerate(((k_hbm, k), (v_hbm, v), (q_hbm, q)))
     ]
-    for copy in loads:
-        copy.start()
-    pl.semaphore_wait(barrier, nb - 1 + nm - 1)
+    pl.semaphore_wait(barrier, nz - 1 + nx - 1 + nm - 1)
+    for t in row:
+        pl.semaphore_signal(row_sem, inc=1, device_id=(t, m), device_id_type=MESH)
 
     for c in range(CHUNKS):
         for t in peers:
+            if c == 0 and t is rest[0]:
+                pl.semaphore_wait(row_sem, nx - 1)
             pltpu.make_async_remote_copy(
                 src_ref=state_hbm.at[convs(c), piece(t), :], dst_ref=gath[c].at[me],
                 send_sem=a_sem.at[0, c], recv_sem=a_sem.at[1, c],
@@ -80,6 +88,9 @@
         pltpu.make_async_copy(
             state_hbm.at[convs(c), piece(me), :], gath[c].at[me], a_sem.at[1, c]
         ).start()
+        if c == 0:
+            for copy in loads:
+                copy.start()
 
     for copy in loads[:4]:
         copy.wait()
@@ -129,20 +140,20 @@
     for c in range(CHUNKS):
         wait_bytes(gath[c], a_sem.at[1, c])
 
-        def pick(d, _):
-            for jj in range(PER):
-                outg[c, d, jj] = gath[c][src_ref[0, d * CONV + c * PER + jj], jj]
-            return 0
-
-        lax.fori_loop(0, nb, pick, 0, unroll=4)
+        def pick(t):
+            for jj in range(SIZES[c]):
+                outg[c][t, jj] = gath[c][src_ref[0, t * CONV + STARTS[c] + jj], jj]
+
         for t in peers:
+            pick(t)
             pltpu.make_async_remote_copy(
-                src_ref=outg.at[c, t], dst_ref=carr.at[convs(c), piece(me), :],
+                src_ref=outg[c].at[t], dst_ref=carr.at[convs(c), piece(me), :],
                 send_sem=b_sem.at[0, c], recv_sem=b_sem.at[1, c],
                 device_id=(t, m), device_id_type=MESH,
             ).start()
+        pick(me)
         pltpu.make_async_copy(
-            outg.at[c, me], carr.at[convs(c), piece(me), :], b_sem.at[1, c]
+            outg[c].at[me], carr.at[convs(c), piece(me), :], b_sem.at[1, c]
         ).start()
 
     def read_carried(j):
@@ -153,8 +164,8 @@
 
     def finish(c):
         wait_bytes(carr.at[convs(c)], b_sem.at[1, c])
-        for jj in range(PER):
-            j = c * PER + jj
+        for jj in range(SIZES[c]):
+            j = STARTS[c] + jj
             live = row_i < len_ref[j]
             read_carried(j)
             square = jnp.zeros((TURN, HD), jnp.float32)
@@ -172,16 +183,16 @@
                 jnp.ones((8, 2 * HD), jnp.bfloat16), jnp.concatenate([high, low], axis=1),
                 (((1,), (1,)), ((), ())), preferred_element_type=jnp.float32,
             )
-            sums[c, m, pl.ds(jj, 1), :] = row[0:1]
-        for d in range(1, nm):
+            sums[c][m, pl.ds(jj, 1), :] = row[0:1]
+        for d in sorted(range(1, nm), key=lambda d: -min(d, nm - d)):
             pltpu.make_async_remote_copy(
-                src_ref=sums.at[c, m], dst_ref=sums.at[c, m], send_sem=m_sem.at[0, c],
+                src_ref=sums[c].at[m], dst_ref=sums[c].at[m], send_sem=m_sem.at[0, c],
                 recv_sem=m_sem.at[1, c], device_id=(me, lax.rem(m + d, nm)), device_id_type=MESH,
             ).start()
 
     def update(c):
-        for jj in range(PER):
-            j = c * PER + jj
+        for jj in range(SIZES[c]):
+            j = STARTS[c] + jj
             length = len_ref[j].astype(jnp.float32)
             read_carried(j)
             for h in range(HEADS):
@@ -190,11 +201,11 @@
             sout[j] = wide[1].astype(jnp.bfloat16)
 
     def normalize(c):
-        wait_bytes(sums.at[c, pl.ds(0, nm - 1)], m_sem.at[1, c])
-        for jj in range(PER):
-            j = c * PER + jj
+        wait_bytes(sums[c].at[pl.ds(0, nm - 1)], m_sem.at[1, c])
+        for jj in range(SIZES[c]):
+            j = STARTS[c] + jj
             total = lax.dot_general(
-                sums[c, :, jj, :], jnp.ones((nm, HD), jnp.float32), (((0,), (0,)), ((), ())),
+                sums[c][:, jj, :], jnp.ones((nm, HD), jnp.float32), (((0,), (0,)), ((), ())),
                 preferred_element_type=jnp.float32, precision=HIGH,
             )
             scale = lax.rsqrt(total / (nm * WIDTH) + EPS)
@@ -211,8 +222,8 @@
 
     for c in range(CHUNKS):
         wait_bytes(gath[c].at[pl.ds(0, nb - 1)], a_sem.at[0, c])
-        wait_bytes(outg.at[c, pl.ds(0, nb - 1)], b_sem.at[0, c])
-        wait_bytes(sums.at[c, pl.ds(0, nm - 1)], m_sem.at[0, c])
+        wait_bytes(outg[c].at[pl.ds(0, nb - 1)], b_sem.at[0, c])
+        wait_bytes(sums[c].at[pl.ds(0, nm - 1)], m_sem.at[0, c])
 
 
 def store_kernel(out, sout, out_hbm, sout_hbm, sems):
@@ -264,15 +275,15 @@
             pltpu.VMEM((CONV, HEADS, HD, HD), f32),
             pltpu.VMEM((HEADS, TURN, TURN), f32),
             pltpu.VMEM((HEADS, TURN, HD), f32),
-            pltpu.VMEM((CHUNKS, nb, PER, rows, HD), bf16),
             pltpu.VMEM((CONV, ROWS, HD), bf16),
             pltpu.VMEM((2, ROWS, HD), f32),
-            pltpu.VMEM((CHUNKS, nm, PER, TURN), f32),
             pltpu.SemaphoreType.DMA((5,)),
             pltpu.SemaphoreType.DMA((3,)),
         ]
         + [pltpu.SemaphoreType.DMA((2, CHUNKS))] * 3
-        + [pltpu.VMEM((nb, PER, rows, HD), bf16)] * CHUNKS,
+        + [pltpu.SemaphoreType.REGULAR]
+        + [pltpu.VMEM((nb, n, rows, HD), bf16) for n in SIZES * 2]
+        + [pltpu.VMEM((nm, n, TURN), f32) for n in SIZES],
         compiler_params=pltpu.CompilerParams(
             collective_id=0, has_side_effects=True, vmem_limit_bytes=40 << 20
         ),

time: 49.8 us -> 49.4 us (level)
  no operation moved by 1% of the time
where the time goes in v3:
time: 49.4 us; the launch traced here: 49.3 us
  Pallas kernels  48.7 us (99%)
  between operations  0.64 us (1%)
    pallas_call x1, Pallas kernels, per_device(): pl.pallas_call(functools.partial(kernel, nx, nz, nm), out_shape=(pltpu.VM...  47.5 us
    pallas_call x1, Pallas kernels, per_device(): pl.pallas_call(store_kernel, out_shape=(jax.ShapeDtypeStruct((CONV, TURN,...  1.16 us

profile of v3, /device:TPU:1, one launch (start us, length us, event | category | flops | bytes accessed | tf_op | source)
XLA Modules:
  0.0 49.3 jit_solution(13967299515740364556)
XLA Ops:
  0.6 47.5 %shard_map.95 = (bf16[4,256,512]{2,1,0:T(8,128)(2,1)S(1)}, bf16[4,512,128]{2,1,0:T(8,128)(2,1)S(1)}) custom-call(f32[4]{0:T(128)} %decay_hbm.1, s32[4]{0:T(128)} %len_hbm.1, s32[1,128]{1,0:T(1,128)} %bitcast.14, f32[1,512]{1,0:T(1,128)} %bitcast.13, bf16[4,256,512]{2,1,0:T(8,128)(2,1)} %q_hbm.1, bf16[4,256,512]{2,1,0:T(8,128)(2,1)} %k_hbm.1, ...), custom_call_target="tpu_custom_call" | custom-call | tf_op jit(solution)/shard_map/pallas_call | solution.py:256
  48.2 1.2 %shard_map.96 = (bf16[4,256,512]{2,1,0:T(8,128)(2,1)}, bf16[4,512,128]{2,1,0:T(8,128)(2,1)}) custom-call(bf16[4,256,512]{2,1,0:T(8,128)(2,1)S(1)} %get-tuple-element.6.out, bf16[4,512,128]{2,1,0:T(8,128)(2,1)S(1)} %get-tuple-element.7.sout), custom_call_target="tpu_custom_call" | custom-call | tf_op jit(solution)/shard_map/pallas_call | solution.py:291
